TPU v7x, 32 devices: a whole 2x2x4 slice. The times are simulated.
32 devices in a mesh: seq: 4 (over y, x), chan: 4 (over z), rep: 2 (over core).
Axes of the slice: x: 2, y: 2, z: 4, core: 2. Of those that a mesh axis runs over, the one named last changes fastest.
Arguments:
- tokens: bfloat16 [3072, 8192], P(('rep', 'seq'), 'chan'), parts along dimension 0, may hold values from -6 to 6
- w_in: bfloat16 [1024, 3, 8192], P('chan', None, 'seq'), may hold values from -0.0625 to 0.0625
- short_taps: float32 [3, 3, 1024], P(None, None, 'chan'), may hold values from -3 to 3
- decay: float32 [16, 1024], P(None, 'chan'), may hold values from 0.00016276042 to 0.03
- residue: float32 [16, 1024], P(None, 'chan'), may hold values from -2 to 2
- skip: float32 [1024], P('chan'), may hold values from -2.5 to 2.5
- w_out: bfloat16 [1024, 8192], P(None, 'chan'), may hold values from -0.1875 to 0.1875
Outputs:
- mixed: bfloat16 [3072, 8192], P(('rep', 'seq'), 'chan'), parts along dimension 0
There are 2 independent parts, one for each index of `rep`. A program takes and returns all parts, laid end to end along the dimension named above; an argument that names none is the same for every part. Nothing has to cross between parts.
All inputs are finite; a program needn't handle non-finite values.
Results may differ from a plain program's by a relative error of at most 0.0079.
Values may be sent and summed in bfloat16 or wider, within the bound.
A program may use at most 128 MiB of HBM per device.

v0:
```python
import functools

import jax
import jax.numpy as jnp
from jax import lax
from jax.experimental import pallas as pl
from jax.experimental.pallas import tpu as pltpu
from jax.sharding import PartitionSpec as P

MESH = pl.DeviceIdType.MESH
F32 = jnp.float32
BF16 = jnp.bfloat16
STEP = 16
HALO = 16


def kernel(
    dims,
    tok_hbm, w_hbm, taps_ref, decay_ref, residue_ref, skip_ref, wout_hbm,
    out_ref,
    tokbuf, wbuf, woutbuf, acc, qbuf, hsend, hrecv, zbuf, query, ubuf, ssend, srecv,
    t_in, t_out, t_loc, gbuf, acc2,
    loc_sem, tsend_sem, trecv_sem, wsend_sem, wrecv_sem, xsend_sem, xrecv_sem,
    hsend_sem, hrecv_sem, ssend_sem, srecv_sem, gsend_sem, grecv_sem,
):
    n_seq, n_chan, n_rep, parts, wparts, rows, ch = dims
    modes = decay_ref.shape[0]
    half = wbuf.shape[2]
    s = lax.axis_index("seq")
    c = lax.axis_index("chan")
    r = lax.axis_index("rep")
    blocks = rows // STEP

    barrier = pltpu.get_barrier_semaphore()
    for o in range(1, n_seq):
        pl.semaphore_signal(
            barrier, inc=1, device_id={"seq": lax.rem(s + o, n_seq)}, device_id_type=MESH
        )
    for o in range(1, n_rep):
        pl.semaphore_signal(
            barrier, inc=1, device_id={"rep": lax.rem(r + o, n_rep)}, device_id_type=MESH
        )

    @pl.when(c > 0)
    def _():
        pl.semaphore_signal(barrier, inc=1, device_id={"chan": c - 1}, device_id_type=MESH)

    @pl.when(c < n_chan - 1)
    def _():
        pl.semaphore_signal(barrier, inc=1, device_id={"chan": c + 1}, device_id_type=MESH)

    own_tok = pltpu.make_async_copy(tok_hbm, tokbuf.at[c], loc_sem.at[0])
    own_w = pltpu.make_async_copy(
        w_hbm, wbuf.at[:, pl.ds(s * wparts, wparts)], loc_sem.at[1]
    )
    own_wout = pltpu.make_async_copy(wout_hbm, woutbuf, loc_sem.at[2])
    own_tok.start()
    own_w.start()
    own_wout.start()

    peers = n_seq - 1 + n_rep - 1
    at_end = (c == 0) | (c == n_chan - 1)

    @pl.when(at_end)
    def _():
        pl.semaphore_wait(barrier, peers + min(1, n_chan - 1))

    @pl.when(jnp.logical_not(at_end))
    def _():
        pl.semaphore_wait(barrier, peers + 2)

    def tok_copy(block, k, way, own):
        src = tok_hbm.at[k] if own else tokbuf.at[block, k]
        return pltpu.make_async_remote_copy(
            src_ref=src,
            dst_ref=tokbuf.at[block, k],
            send_sem=tsend_sem.at[way, block, k],
            recv_sem=trecv_sem.at[block, k],
            device_id={"chan": c + (1 if way == 0 else -1)},
            device_id_type=MESH,
        )

    def can_send(way):
        return c < n_chan - 1 if way == 0 else c > 0

    def source(way, d):
        block = c - d if way == 0 else c + d
        there = block >= 0 if way == 0 else block <= n_chan - 1
        return block, there

    for k in range(parts):
        for way in range(2):
            @pl.when(can_send(way))
            def _():
                tok_copy(c, k, way, True).start()

    def w_copy(o, incoming):
        to = lax.rem(s + o, n_seq)
        block = lax.rem(s + n_seq - o, n_seq) if incoming else s
        return pltpu.make_async_remote_copy(
            src_ref=w_hbm.at[r],
            dst_ref=wbuf.at[r, pl.ds(block * wparts, wparts)],
            send_sem=wsend_sem.at[o],
            recv_sem=wrecv_sem.at[o],
            device_id={"seq": to},
            device_id_type=MESH,
        )

    for o in range(1, n_seq):
        w_copy(o, False).start()

    def x_copy(o, p, incoming):
        block = lax.rem(s + n_seq - o, n_seq)
        which = lax.rem(r + n_rep - p, n_rep) if incoming else r
        place = wbuf.at[which, pl.ds(block * wparts, wparts)]
        return pltpu.make_async_remote_copy(
            src_ref=place,
            dst_ref=place,
            send_sem=xsend_sem.at[o, p],
            recv_sem=xrecv_sem.at[o, p],
            device_id={"rep": lax.rem(r + p, n_rep)},
            device_id_type=MESH,
        )

    rate = decay_ref[...]
    amp = residue_ref[...] * jnp.sqrt(rate)
    step_of = lax.broadcasted_iota(jnp.int32, (STEP, ch), 0)
    for m in range(modes):
        t_out[m] = amp[m : m + 1] * jnp.exp(-rate[m : m + 1] * step_of.astype(F32))
    filt = t_out[0]
    for m in range(1, modes):
        filt = filt + t_out[m]
    for i in range(STEP):
        t_in[i] = jnp.exp(-rate * float(STEP - i))
        if i == 0:
            t_loc[i] = filt
        else:
            t_loc[i] = jnp.concatenate([jnp.zeros((i, ch), F32), filt[: STEP - i]], axis=0)
    acc[...] = jnp.zeros_like(acc)

    def arrive(d, then):
        for k in range(parts):
            for way in range(2):
                block, there = source(way, d)

                @pl.when(there)
                def _():
                    tok_copy(block, k, way, False).wait_recv()

                    if d < n_chan - 1:
                        @pl.when(can_send(way))
                        def _():
                            tok_copy(block, k, way, False).start()

                    if then:
                        multiply(block, k)

    def multiply(block, k):
        j = block * parts + k
        a = tokbuf[block, k]
        for h in range(n_rep):
            acc[:, h * half : (h + 1) * half] += lax.dot_general(
                a, wbuf[h, j], (((1,), (1,)), ((), ())), preferred_element_type=F32
            )

    for d in range(1, n_chan - 1):
        arrive(d, False)
    for o in range(1, n_seq):
        w_copy(o, True).wait_recv()
        for p in range(1, n_rep):
            x_copy(o, p, False).start()
    own_tok.wait()
    own_w.wait()
    for o in range(1, n_seq):
        for p in range(1, n_rep):
            x_copy(o, p, True).wait_recv()

    def early(i, carry):
        block = i // parts
        k = lax.rem(i, parts)
        off = block - c

        @pl.when((off < n_chan - 1) & (off > 1 - n_chan))
        def _():
            multiply(block, k)

        return carry

    lax.fori_loop(0, n_chan * parts, early, 0)
    if n_chan > 1:
        arrive(n_chan - 1, True)

    qbuf[HALO:, :] = acc[...].astype(BF16).astype(F32)
    hsend[...] = qbuf[rows:, :].astype(BF16)
    halo_copy = pltpu.make_async_remote_copy(
        src_ref=hsend,
        dst_ref=hrecv,
        send_sem=hsend_sem,
        recv_sem=hrecv_sem,
        device_id={"seq": lax.rem(s + 1, n_seq)},
        device_id_type=MESH,
    )

    @pl.when(s < n_seq - 1)
    def _():
        halo_copy.start()

    @pl.when(s > 0)
    def _():
        halo_copy.wait_recv()
        qbuf[:HALO, :] = hrecv[...].astype(F32)

    @pl.when(s == 0)
    def _():
        qbuf[:HALO, :] = jnp.zeros((HALO, 3 * ch), F32)

    leap = jnp.exp(-rate * float(STEP))

    def first(b, state):
        base = pl.multiple_of(b * STEP, STEP)
        feats = []
        for g in range(3):
            window = qbuf[pl.ds(base + 8, STEP + 8), g * ch : (g + 1) * ch]
            feat = taps_ref[g : g + 1] * window[8:]
            for j in range(1, 3):
                row = j * 3 + g
                feat = feat + taps_ref[row : row + 1] * window[8 - j : 8 - j + STEP]
            feats.append(feat)
        z = (feats[1] * feats[2]).astype(BF16).astype(F32)
        query[pl.ds(base, STEP), :] = feats[0]
        zbuf[pl.ds(base, STEP), :] = z
        grown = t_in[0] * z[0:1]
        for i in range(1, STEP):
            grown = grown + t_in[i] * z[i : i + 1]
        ubuf[b] = grown
        return leap * state + grown

    ssend[...] = lax.fori_loop(0, blocks, first, jnp.zeros((modes, ch), F32))

    def s_copy(o):
        return pltpu.make_async_remote_copy(
            src_ref=ssend,
            dst_ref=srecv.at[o],
            send_sem=ssend_sem.at[o],
            recv_sem=srecv_sem.at[o],
            device_id={"seq": lax.rem(s + o, n_seq)},
            device_id_type=MESH,
        )

    for o in range(1, n_seq):
        @pl.when(s + o < n_seq)
        def _():
            s_copy(o).start()

    acc2[:modes, :ch] = jnp.zeros((modes, ch), F32)
    for o in range(1, n_seq):
        @pl.when(s >= o)
        def _():
            s_copy(o).wait_recv()
            acc2[:modes, :ch] += jnp.exp(-rate * float(rows * (o - 1))) * srecv[o]

    skip = skip_ref[...]

    def second(b, state):
        base = pl.multiple_of(b * STEP, STEP)
        z = zbuf[pl.ds(base, STEP), :]
        total = skip * z
        for i in range(STEP):
            total = total + t_loc[i] * z[i : i + 1]
        for m in range(modes):
            total = total + t_out[m] * state[m : m + 1]
        longc = total.astype(BF16).astype(F32)
        gbuf[c, pl.ds(base, STEP), :] = (query[pl.ds(base, STEP), :] * longc).astype(BF16)
        return leap * state + ubuf[b]

    lax.fori_loop(0, blocks, second, acc2[:modes, :ch])

    def g_copy(block, way):
        return pltpu.make_async_remote_copy(
            src_ref=gbuf.at[block],
            dst_ref=gbuf.at[block],
            send_sem=gsend_sem.at[way, block],
            recv_sem=grecv_sem.at[block],
            device_id={"chan": c + (1 if way == 0 else -1)},
            device_id_type=MESH,
        )

    for way in range(2):
        @pl.when(can_send(way))
        def _():
            g_copy(c, way).start()

    own_wout.wait()
    width = acc2.shape[1]
    tile = min(512, width)

    def project(block, opening):
        def one(i, carry):
            cols = pl.ds(pl.multiple_of(i * tile, tile), tile)
            part = jnp.dot(gbuf[block], woutbuf[block, :, cols], preferred_element_type=F32)
            if opening:
                acc2[:, cols] = part
            else:
                acc2[:, cols] += part
            return carry

        lax.fori_loop(0, width // tile, one, 0)

    project(c, True)
    for d in range(1, n_chan):
        for way in range(2):
            block, there = source(way, d)

            @pl.when(there)
            def _():
                g_copy(block, way).wait_recv()

                if d < n_chan - 1:
                    @pl.when(can_send(way))
                    def _():
                        g_copy(block, way).start()

                project(block, False)
    out_ref[...] = acc2[...].astype(BF16)

    for d in range(n_chan - 1):
        for way in range(2):
            block, there = source(way, d)

            @pl.when(there & can_send(way))
            def _():
                for k in range(parts):
                    tok_copy(block, k, way, d == 0).wait_send()
                g_copy(block, way).wait_send()

    for o in range(1, n_seq):
        w_copy(o, False).wait_send()
        for p in range(1, n_rep):
            x_copy(o, p, False).wait_send()

        @pl.when(s + o < n_seq)
        def _():
            s_copy(o).wait_send()

    @pl.when(s < n_seq - 1)
    def _():
        halo_copy.wait_send()


def on_device(tokens, w_in, short_taps, decay, residue, skip, w_out):
    n_seq, n_chan, n_rep = (lax.axis_size(a) for a in ("seq", "chan", "rep"))
    rows, depth = tokens.shape
    ch, branches, wdepth = w_in.shape
    modes = decay.shape[0]
    width = w_out.shape[1]
    piece = min(depth // 4, wdepth)
    parts, wparts = depth // piece, wdepth // piece
    half = branches * ch // n_rep
    tok = tokens.reshape(rows, parts, piece).transpose(1, 0, 2)
    w = w_in.reshape(ch, branches, wparts, piece).transpose(2, 1, 0, 3)
    w = w.reshape(wparts, n_rep, half, piece).transpose(1, 0, 2, 3)
    taps = short_taps.reshape(short_taps.shape[0] * branches, ch)
    dims = (n_seq, n_chan, n_rep, parts, wparts, rows, ch)
    vmem = pl.BlockSpec(memory_space=pltpu.VMEM)
    hbm = pl.BlockSpec(memory_space=pl.ANY)
    dma = pltpu.SemaphoreType.DMA
    return pl.pallas_call(
        functools.partial(kernel, dims),
        out_shape=jax.ShapeDtypeStruct((rows, width), BF16),
        in_specs=[hbm, hbm, vmem, vmem, vmem, vmem, hbm],
        out_specs=vmem,
        scratch_shapes=[
            pltpu.VMEM((n_chan, parts, rows, piece), BF16),
            pltpu.VMEM((n_rep, n_seq * wparts, half, piece), BF16),
            pltpu.VMEM((n_chan, ch, width), BF16),
            pltpu.VMEM((rows, branches * ch), F32),
            pltpu.VMEM((rows + HALO, branches * ch), F32),
            pltpu.VMEM((HALO, branches * ch), BF16),
            pltpu.VMEM((HALO, branches * ch), BF16),
            pltpu.VMEM((rows, ch), F32),
            pltpu.VMEM((rows, ch), F32),
            pltpu.VMEM((rows // STEP, modes, ch), F32),
            pltpu.VMEM((modes, ch), F32),
            pltpu.VMEM((n_seq, modes, ch), F32),
            pltpu.VMEM((STEP, modes, ch), F32),
            pltpu.VMEM((modes, STEP, ch), F32),
            pltpu.VMEM((STEP, STEP, ch), F32),
            pltpu.VMEM((n_chan, rows, ch), BF16),
            pltpu.VMEM((rows, width), F32),
            dma((3,)),
            dma((2, n_chan, parts)),
            dma((n_chan, parts)),
            dma((n_seq,)),
            dma((n_seq,)),
            dma((n_seq, n_rep)),
            dma((n_seq, n_rep)),
            dma(()),
            dma(()),
            dma((n_seq,)),
            dma((n_seq,)),
            dma((2, n_chan)),
            dma((n_chan,)),
        ],
        compiler_params=pltpu.CompilerParams(
            collective_id=0, has_side_effects=True, vmem_limit_bytes=56 * 1024 * 1024
        ),
        cost_estimate=pl.CostEstimate(
            flops=2 * rows * (n_chan * depth * branches * ch + n_chan * ch * width),
            bytes_accessed=2 * (rows * depth + branches * ch * wdepth + n_chan * ch * width),
            transcendentals=0,
        ),
    )(tok, w, taps, decay, residue, skip.reshape(1, ch), w_out.reshape(n_chan, ch, width))


def solution(mesh):
    placed = (
        P(("rep", "seq"), "chan"),
        P("chan", None, "seq"),
        P(None, None, "chan"),
        P(None, "chan"),
        P(None, "chan"),
        P("chan"),
        P(None, "chan"),
    )
    return jax.shard_map(
        on_device, mesh=mesh, in_specs=placed, out_specs=P(("rep", "seq"), "chan"), check_vma=False
    )
```

profile of v0, /device:TPU:4, one launch (start us, length us, event | category | flops | bytes accessed | tf_op | source)
XLA Modules:
  0.0 150.9 jit_solution(17046092417243414664)
XLA Ops:
  0.0 4.7 %copy.13 = bf16[256,3,2048]{0,2,1:T(8,128)(2,1)} copy(bf16[256,3,2048]{2,0,1:T(8,128)(2,1)} %param.8) | data formatting | bytes 6291456 | tf_op args[1]
  4.7 3.2 %copy.14 = bf16[4,3,256,512]{3,2,1,0:T(8,128)(2,1)S(1)} copy(bf16[4,3,256,512]{2,3,0,1:T(8,128)(2,1)} %bitcast.12) | data formatting | bytes 6291456 | tf_op jit(solution)/shard_map/transpose | solution.py:360
  7.9 2.0 %copy.17 = bf16[4,2,384,512]{3,2,0,1:T(8,128)(2,1)} copy(bf16[4,2,384,512]{3,2,1,0:T(8,128)(2,1)S(1)} %bitcast.11) | data formatting | bytes 6291456 | tf_op jit(solution)/shard_map/reshape | solution.py:361
  9.9 0.0 copy-start
  9.9 1.9 %copy.11 = bf16[384,2048]{0,1:T(8,128)(2,1)S(1)} copy(bf16[384,2048]{1,0:T(8,128)(2,1)} %param.7) | data formatting | bytes 3145728 | tf_op args[0]
  11.8 1.6 %copy.12 = bf16[384,4,512]{2,0,1:T(8,128)(2,1)} copy(bf16[384,4,512]{0,2,1:T(8,128)(2,1)S(1)} %bitcast.13) | data formatting | bytes 3145728 | tf_op jit(solution)/shard_map/reshape | solution.py:359
  13.4 0.0 copy-done
  13.4 0.6 reshape.21.taps_ref
  14.0 134.1 %shard_map.73 = bf16[384,2048]{1,0:T(8,128)(2,1)} custom-call(bf16[4,384,512]{2,1,0:T(8,128)(2,1)} %bitcast.15, bf16[2,4,384,512]{3,2,1,0:T(8,128)(2,1)} %bitcast.14, f32[9,256]{1,0:T(8,128)} %reshape.21.taps_ref, f32[16,256]{1,0:T(8,128)} %decay_ref.1, f32[16,256]{1,0:T(8,128)} %residue_ref.1, f32[1,256]{1,0:T(1,128)} %bitcast.17, ...), custom_call_target="tpu_custom_call" | custom-call | flops 6442450944 | bytes 8912896 | tf_op jit(solution)/shard_map/pallas_call | solution.py:367
  148.1 2.7 %copy.19 = bf16[384,2048]{1,0:T(8,128)(2,1)} copy(bf16[384,2048]{1,0:T(8,128)(2,1)} %shard_map.73) | data formatting | bytes 3145728
Async XLA Ops:
  9.9 3.5 %copy-start = (f32[3,3,256]{2,1,0:T(4,128)S(1)}, f32[3,3,256]{2,1,0:T(4,128)}, u32[]{:S(2)}) copy-start(f32[3,3,256]{2,1,0:T(4,128)} %param.9) | copy-start | bytes 27652
where the time goes:
time: 151 us
  Pallas kernels  134 us (89%)
  local copies, waits for them, and re-layouts  16.7 us (11%)
    pallas_call x1, Pallas kernels, on_device(): pl.pallas_call(functools.partial(kernel, dims), out_shape=jax.ShapeDtypeS...  134 us
    unnamed x5, local copies, waits for them, and re-layouts  9.29 us
    transpose x1, local copies, waits for them, and re-layouts, on_device(): w = w_in.reshape(ch, branches, wparts, piece).transpose(2, 1, 0, 3)  3.2 us

commit v1 on v0

--- a/solution.py
+++ b/solution.py
@@ -18,14 +18,17 @@
     dims,
     tok_hbm, w_hbm, taps_ref, decay_ref, residue_ref, skip_ref, wout_hbm,
     out_ref,
-    tokbuf, wbuf, woutbuf, acc, qbuf, hsend, hrecv, zbuf, query, ubuf, ssend, srecv,
+    tokbuf, wbuf, woutbuf, acc, qbuf, hsend, hrecv, local, query, ubuf, ssend, srecv,
     t_in, t_out, t_loc, gbuf, acc2,
     loc_sem, tsend_sem, trecv_sem, wsend_sem, wrecv_sem, xsend_sem, xrecv_sem,
     hsend_sem, hrecv_sem, ssend_sem, srecv_sem, gsend_sem, grecv_sem,
 ):
-    n_seq, n_chan, n_rep, parts, wparts, rows, ch = dims
+    n_seq, n_chan, n_rep, parts, piece, rows, ch = dims
     modes = decay_ref.shape[0]
-    half = wbuf.shape[2]
+    half, wdepth = wbuf.shape[2:]
+    depth = tokbuf.shape[2]
+    group = rows // parts
+    order = [parts - 1] + list(range(parts - 1))
     s = lax.axis_index("seq")
     c = lax.axis_index("chan")
     r = lax.axis_index("rep")
@@ -50,12 +53,13 @@
         pl.semaphore_signal(barrier, inc=1, device_id={"chan": c + 1}, device_id_type=MESH)
 
     own_tok = pltpu.make_async_copy(tok_hbm, tokbuf.at[c], loc_sem.at[0])
-    own_w = pltpu.make_async_copy(
-        w_hbm, wbuf.at[:, pl.ds(s * wparts, wparts)], loc_sem.at[1]
-    )
-    own_wout = pltpu.make_async_copy(wout_hbm, woutbuf, loc_sem.at[2])
+    own_w = [
+        pltpu.make_async_copy(w_hbm.at[h], wbuf.at[h, s], loc_sem.at[2 + h]) for h in range(n_rep)
+    ]
+    own_wout = pltpu.make_async_copy(wout_hbm, woutbuf, loc_sem.at[1])
     own_tok.start()
-    own_w.start()
+    for copy in own_w:
+        copy.start()
     own_wout.start()
 
     peers = n_seq - 1 + n_rep - 1
@@ -70,10 +74,10 @@
         pl.semaphore_wait(barrier, peers + 2)
 
     def tok_copy(block, k, way, own):
-        src = tok_hbm.at[k] if own else tokbuf.at[block, k]
+        span = pl.ds(k * group, group)
         return pltpu.make_async_remote_copy(
-            src_ref=src,
-            dst_ref=tokbuf.at[block, k],
+            src_ref=tok_hbm.at[span] if own else tokbuf.at[block, span],
+            dst_ref=tokbuf.at[block, span],
             send_sem=tsend_sem.at[way, block, k],
             recv_sem=trecv_sem.at[block, k],
             device_id={"chan": c + (1 if way == 0 else -1)},
@@ -88,7 +92,7 @@
         there = block >= 0 if way == 0 else block <= n_chan - 1
         return block, there
 
-    for k in range(parts):
+    for k in order:
         for way in range(2):
             @pl.when(can_send(way))
             def _():
@@ -99,7 +103,7 @@
         block = lax.rem(s + n_seq - o, n_seq) if incoming else s
         return pltpu.make_async_remote_copy(
             src_ref=w_hbm.at[r],
-            dst_ref=wbuf.at[r, pl.ds(block * wparts, wparts)],
+            dst_ref=wbuf.at[r, block],
             send_sem=wsend_sem.at[o],
             recv_sem=wrecv_sem.at[o],
             device_id={"seq": to},
@@ -112,7 +116,7 @@
     def x_copy(o, p, incoming):
         block = lax.rem(s + n_seq - o, n_seq)
         which = lax.rem(r + n_rep - p, n_rep) if incoming else r
-        place = wbuf.at[which, pl.ds(block * wparts, wparts)]
+        place = wbuf.at[which, block]
         return pltpu.make_async_remote_copy(
             src_ref=place,
             dst_ref=place,
@@ -138,8 +142,24 @@
             t_loc[i] = jnp.concatenate([jnp.zeros((i, ch), F32), filt[: STEP - i]], axis=0)
     acc[...] = jnp.zeros_like(acc)
 
-    def arrive(d, then):
-        for k in range(parts):
+    def multiply(block, span, h):
+        def one(i, carry):
+            off = pl.multiple_of(i * piece, piece)
+            at = block * depth + off
+            cols = pl.ds(pl.multiple_of(lax.rem(at, wdepth), piece), piece)
+            outs = pl.ds(pl.multiple_of(h * half, 128), half)
+            acc[span, outs] += lax.dot_general(
+                tokbuf[block, span, pl.ds(off, piece)],
+                wbuf[h, at // wdepth, :, cols],
+                (((1,), (1,)), ((), ())),
+                preferred_element_type=F32,
+            )
+            return carry
+
+        lax.fori_loop(0, depth // piece, one, 0)
+
+    for d in range(1, n_chan - 1):
+        for k in order:
             for way in range(2):
                 block, there = source(way, d)
 
@@ -147,51 +167,36 @@
                 def _():
                     tok_copy(block, k, way, False).wait_recv()
 
-                    if d < n_chan - 1:
-                        @pl.when(can_send(way))
-                        def _():
-                            tok_copy(block, k, way, False).start()
-
-                    if then:
-                        multiply(block, k)
-
-    def multiply(block, k):
-        j = block * parts + k
-        a = tokbuf[block, k]
-        for h in range(n_rep):
-            acc[:, h * half : (h + 1) * half] += lax.dot_general(
-                a, wbuf[h, j], (((1,), (1,)), ((), ())), preferred_element_type=F32
-            )
-
-    for d in range(1, n_chan - 1):
-        arrive(d, False)
+                    @pl.when(can_send(way))
+                    def _():
+                        tok_copy(block, k, way, False).start()
+
     for o in range(1, n_seq):
         w_copy(o, True).wait_recv()
         for p in range(1, n_rep):
             x_copy(o, p, False).start()
     own_tok.wait()
-    own_w.wait()
-    for o in range(1, n_seq):
-        for p in range(1, n_rep):
+    for copy in own_w:
+        copy.wait()
+
+    def early(h):
+        def one(block, carry):
+            off = block - c
+
+            @pl.when((off < max(1, n_chan - 1)) & (off > -max(1, n_chan - 1)))
+            def _():
+                multiply(block, pl.ds(0, rows), h)
+
+            return carry
+
+        lax.fori_loop(0, n_chan, one, 0)
+
+    early(r)
+    for p in range(1, n_rep):
+        for o in range(1, n_seq):
             x_copy(o, p, True).wait_recv()
-
-    def early(i, carry):
-        block = i // parts
-        k = lax.rem(i, parts)
-        off = block - c
-
-        @pl.when((off < n_chan - 1) & (off > 1 - n_chan))
-        def _():
-            multiply(block, k)
-
-        return carry
-
-    lax.fori_loop(0, n_chan * parts, early, 0)
-    if n_chan > 1:
-        arrive(n_chan - 1, True)
-
-    qbuf[HALO:, :] = acc[...].astype(BF16).astype(F32)
-    hsend[...] = qbuf[rows:, :].astype(BF16)
+        early(lax.rem(r + n_rep - p, n_rep))
+
     halo_copy = pltpu.make_async_remote_copy(
         src_ref=hsend,
         dst_ref=hrecv,
@@ -200,23 +205,9 @@
         device_id={"seq": lax.rem(s + 1, n_seq)},
         device_id_type=MESH,
     )
-
-    @pl.when(s < n_seq - 1)
-    def _():
-        halo_copy.start()
-
-    @pl.when(s > 0)
-    def _():
-        halo_copy.wait_recv()
-        qbuf[:HALO, :] = hrecv[...].astype(F32)
-
-    @pl.when(s == 0)
-    def _():
-        qbuf[:HALO, :] = jnp.zeros((HALO, 3 * ch), F32)
-
-    leap = jnp.exp(-rate * float(STEP))
-
-    def first(b, state):
+    skip = skip_ref[...]
+
+    def first(b, carry):
         base = pl.multiple_of(b * STEP, STEP)
         feats = []
         for g in range(3):
@@ -228,14 +219,56 @@
             feats.append(feat)
         z = (feats[1] * feats[2]).astype(BF16).astype(F32)
         query[pl.ds(base, STEP), :] = feats[0]
-        zbuf[pl.ds(base, STEP), :] = z
         grown = t_in[0] * z[0:1]
+        total = skip * z + t_loc[0] * z[0:1]
         for i in range(1, STEP):
             grown = grown + t_in[i] * z[i : i + 1]
+            total = total + t_loc[i] * z[i : i + 1]
         ubuf[b] = grown
-        return leap * state + grown
-
-    ssend[...] = lax.fori_loop(0, blocks, first, jnp.zeros((modes, ch), F32))
+        local[pl.ds(base, STEP), :] = total
+        return carry
+
+    per = group // STEP
+    for k in order:
+        span = pl.ds(k * group, group)
+        if n_chan > 1:
+            for way in range(2):
+                block, there = source(way, n_chan - 1)
+
+                @pl.when(there)
+                def _():
+                    tok_copy(block, k, way, False).wait_recv()
+                    for h in range(n_rep):
+                        multiply(block, span, h)
+
+        qbuf[HALO + k * group : HALO + (k + 1) * group, :] = acc[span, :].astype(BF16).astype(F32)
+        if k == parts - 1:
+            hsend[...] = qbuf[rows:, :].astype(BF16)
+
+            @pl.when(s < n_seq - 1)
+            def _():
+                halo_copy.start()
+
+            lax.fori_loop(k * per + 1, blocks, first, 0)
+        else:
+            if k == 0:
+                @pl.when(s > 0)
+                def _():
+                    halo_copy.wait_recv()
+                    qbuf[:HALO, :] = hrecv[...].astype(F32)
+
+                @pl.when(s == 0)
+                def _():
+                    qbuf[:HALO, :] = jnp.zeros((HALO, 3 * ch), F32)
+
+            lax.fori_loop(k * per, (k + 1) * per + (1 if k == parts - 2 else 0), first, 0)
+
+    leap = jnp.exp(-rate * float(STEP))
+
+    def scan(b, state):
+        return leap * state + ubuf[b]
+
+    ssend[...] = lax.fori_loop(0, blocks, scan, jnp.zeros((modes, ch), F32))
 
     def s_copy(o):
         return pltpu.make_async_remote_copy(
@@ -259,36 +292,33 @@
             s_copy(o).wait_recv()
             acc2[:modes, :ch] += jnp.exp(-rate * float(rows * (o - 1))) * srecv[o]
 
-    skip = skip_ref[...]
-
     def second(b, state):
         base = pl.multiple_of(b * STEP, STEP)
-        z = zbuf[pl.ds(base, STEP), :]
-        total = skip * z
-        for i in range(STEP):
-            total = total + t_loc[i] * z[i : i + 1]
+        total = local[pl.ds(base, STEP), :]
         for m in range(modes):
             total = total + t_out[m] * state[m : m + 1]
         longc = total.astype(BF16).astype(F32)
         gbuf[c, pl.ds(base, STEP), :] = (query[pl.ds(base, STEP), :] * longc).astype(BF16)
         return leap * state + ubuf[b]
 
-    lax.fori_loop(0, blocks, second, acc2[:modes, :ch])
-
-    def g_copy(block, way):
+    def g_copy(block, k, way):
+        place = gbuf.at[block, pl.ds(k * group, group)]
         return pltpu.make_async_remote_copy(
-            src_ref=gbuf.at[block],
-            dst_ref=gbuf.at[block],
-            send_sem=gsend_sem.at[way, block],
-            recv_sem=grecv_sem.at[block],
+            src_ref=place,
+            dst_ref=place,
+            send_sem=gsend_sem.at[way, block, k],
+            recv_sem=grecv_sem.at[block, k],
             device_id={"chan": c + (1 if way == 0 else -1)},
             device_id_type=MESH,
         )
 
-    for way in range(2):
-        @pl.when(can_send(way))
-        def _():
-            g_copy(c, way).start()
+    state = acc2[:modes, :ch]
+    for k in range(parts):
+        state = lax.fori_loop(k * per, (k + 1) * per, second, state)
+        for way in range(2):
+            @pl.when(can_send(way))
+            def _():
+                g_copy(c, k, way).start()
 
     own_wout.wait()
     width = acc2.shape[1]
@@ -308,19 +338,27 @@
 
     project(c, True)
     for d in range(1, n_chan):
-        for way in range(2):
-            block, there = source(way, d)
-
-            @pl.when(there)
-            def _():
-                g_copy(block, way).wait_recv()
-
-                if d < n_chan - 1:
-                    @pl.when(can_send(way))
-                    def _():
-                        g_copy(block, way).start()
-
-                project(block, False)
+        for k in range(parts):
+            for way in range(2):
+                block, there = source(way, d)
+
+                @pl.when(there)
+                def _():
+                    g_copy(block, k, way).wait_recv()
+
+                    if d < n_chan - 1:
+                        @pl.when(can_send(way))
+                        def _():
+                            g_copy(block, k, way).start()
+
+        for e in range(1, n_chan - 1) if d == n_chan - 2 else [d] if d == n_chan - 1 else []:
+            for way in range(2):
+                block, there = source(way, e)
+
+                @pl.when(there)
+                def _():
+                    project(block, False)
+
     out_ref[...] = acc2[...].astype(BF16)
 
     for d in range(n_chan - 1):
@@ -331,7 +369,7 @@
             def _():
                 for k in range(parts):
                     tok_copy(block, k, way, d == 0).wait_send()
-                g_copy(block, way).wait_send()
+                    g_copy(block, k, way).wait_send()
 
     for o in range(1, n_seq):
         w_copy(o, False).wait_send()
@@ -353,14 +391,12 @@
     ch, branches, wdepth = w_in.shape
     modes = decay.shape[0]
     width = w_out.shape[1]
-    piece = min(depth // 4, wdepth)
-    parts, wparts = depth // piece, wdepth // piece
+    piece = min(512, depth, wdepth)
+    parts = 4
     half = branches * ch // n_rep
-    tok = tokens.reshape(rows, parts, piece).transpose(1, 0, 2)
-    w = w_in.reshape(ch, branches, wparts, piece).transpose(2, 1, 0, 3)
-    w = w.reshape(wparts, n_rep, half, piece).transpose(1, 0, 2, 3)
+    w = w_in.transpose(1, 0, 2).reshape(n_rep, half, wdepth)
     taps = short_taps.reshape(short_taps.shape[0] * branches, ch)
-    dims = (n_seq, n_chan, n_rep, parts, wparts, rows, ch)
+    dims = (n_seq, n_chan, n_rep, parts, piece, rows, ch)
     vmem = pl.BlockSpec(memory_space=pltpu.VMEM)
     hbm = pl.BlockSpec(memory_space=pl.ANY)
     dma = pltpu.SemaphoreType.DMA
@@ -370,8 +406,8 @@
         in_specs=[hbm, hbm, vmem, vmem, vmem, vmem, hbm],
         out_specs=vmem,
         scratch_shapes=[
-            pltpu.VMEM((n_chan, parts, rows, piece), BF16),
-            pltpu.VMEM((n_rep, n_seq * wparts, half, piece), BF16),
+            pltpu.VMEM((n_chan, rows, depth), BF16),
+            pltpu.VMEM((n_rep, n_seq, half, wdepth), BF16),
             pltpu.VMEM((n_chan, ch, width), BF16),
             pltpu.VMEM((rows, branches * ch), F32),
             pltpu.VMEM((rows + HALO, branches * ch), F32),
@@ -387,7 +423,7 @@
             pltpu.VMEM((STEP, STEP, ch), F32),
             pltpu.VMEM((n_chan, rows, ch), BF16),
             pltpu.VMEM((rows, width), F32),
-            dma((3,)),
+            dma((2 + n_rep,)),
             dma((2, n_chan, parts)),
             dma((n_chan, parts)),
             dma((n_seq,)),
@@ -398,8 +434,8 @@
             dma(()),
             dma((n_seq,)),
             dma((n_seq,)),
-            dma((2, n_chan)),
-            dma((n_chan,)),
+            dma((2, n_chan, parts)),
+            dma((n_chan, parts)),
         ],
         compiler_params=pltpu.CompilerParams(
             collective_id=0, has_side_effects=True, vmem_limit_bytes=56 * 1024 * 1024
@@ -409,7 +445,7 @@
             bytes_accessed=2 * (rows * depth + branches * ch * wdepth + n_chan * ch * width),
             transcendentals=0,
         ),
-    )(tok, w, taps, decay, residue, skip.reshape(1, ch), w_out.reshape(n_chan, ch, width))
+    )(tokens, w, taps, decay, residue, skip.reshape(1, ch), w_out.reshape(n_chan, ch, width))
 
 
 def solution(mesh):

time: 151 us -> 133 us (0.88)
  local copies, waits for them, and re-layouts: 16.7 us -> 4.05 us
  Pallas kernels: 134 us -> 128 us
    unnamed x5 -> x1, local copies, waits for them, and re-layouts: 9.29 us -> 2.73 us
    pallas_call x1, Pallas kernels: 134 us -> 128 us  [on_device(): pl.pallas_call(functools.partial(kernel, dims), out_shape=jax.ShapeDtypeS...]
    reshape x2 -> x0, local copies, waits for them, and re-layouts: 3.64 us -> none  [the longest x1 2.01 us: on_device(): w = w.reshape(wparts, n_rep, half, piece).transpose(1, 0, 2, 3)]
    transpose x1 -> x0, local copies, waits for them, and re-layouts: 3.2 us -> none  [on_device(): w = w_in.reshape(ch, branches, wparts, piece).transpose(2, 1, 0, 3)]
where the time goes in v1:
time: 133 us; the launch traced here: 132 us
  Pallas kernels  128 us (96%)
  local copies, waits for them, and re-layouts  4.05 us (3%)
    pallas_call x1, Pallas kernels, on_device(): pl.pallas_call(functools.partial(kernel, dims), out_shape=jax.ShapeDtypeS...  128 us
    unnamed x1, local copies, waits for them, and re-layouts  2.73 us

profile of v1, /device:TPU:4, one launch (start us, length us, event | category | flops | bytes accessed | tf_op | source)
XLA Modules:
  0.0 132.3 jit_solution(17455212440274459606)
XLA Ops:
  0.0 1.3 reshape.13.taps_ref
  1.3 128.2 %shard_map.73 = bf16[384,2048]{1,0:T(8,128)(2,1)} custom-call(bf16[384,2048]{1,0:T(8,128)(2,1)} %tok_hbm.1, bf16[2,384,2048]{2,1,0:T(8,128)(2,1)} %bitcast.6, f32[9,256]{1,0:T(8,128)} %reshape.13.taps_ref, f32[16,256]{1,0:T(8,128)} %decay_ref.1, f32[16,256]{1,0:T(8,128)} %residue_ref.1, f32[1,256]{1,0:T(1,128)} %bitcast.7, bf16[4,256,2048]{2,1,0:T(8,128)(2,1)} %bitcast.5), custom_call_target="tpu_custom_call" | custom-call | flops 6442450944 | bytes 8912896 | tf_op jit(solution)/shard_map/pallas_call | solution.py:403
  129.6 2.7 %copy.9 = bf16[384,2048]{1,0:T(8,128)(2,1)} copy(bf16[384,2048]{1,0:T(8,128)(2,1)} %shard_map.73) | data formatting | bytes 3145728

commit v2 on v1

--- a/solution.py
+++ b/solution.py
@@ -19,8 +19,9 @@
     tok_hbm, w_hbm, taps_ref, decay_ref, residue_ref, skip_ref, wout_hbm,
     out_ref,
     tokbuf, wbuf, woutbuf, acc, qbuf, hsend, hrecv, local, query, ubuf, ssend, srecv,
-    t_in, t_out, t_loc, gbuf, acc2,
+    t_in, t_out, t_loc, gbuf, acc2, pbuf, pacc, psend, precv,
     loc_sem, tsend_sem, trecv_sem, wsend_sem, wrecv_sem, xsend_sem, xrecv_sem,
+    fsend_sem, frecv_sem, ysend_sem, yrecv_sem, psend_sem, precv_sem,
     hsend_sem, hrecv_sem, ssend_sem, srecv_sem, gsend_sem, grecv_sem,
 ):
     n_seq, n_chan, n_rep, parts, piece, rows, ch = dims
@@ -28,6 +29,9 @@
     half, wdepth = wbuf.shape[2:]
     depth = tokbuf.shape[2]
     group = rows // parts
+    proxied = n_chan == 4 and n_seq == n_chan and depth == wdepth
+    wparts = 4 if proxied else 1
+    wpiece = wdepth // wparts
     order = [parts - 1] + list(range(parts - 1))
     s = lax.axis_index("seq")
     c = lax.axis_index("chan")
@@ -98,20 +102,62 @@
             def _():
                 tok_copy(c, k, way, True).start()
 
-    def w_copy(o, incoming):
+    def w_copy(o, q, incoming):
+        cols = pl.ds(q * wpiece, wpiece)
         to = lax.rem(s + o, n_seq)
         block = lax.rem(s + n_seq - o, n_seq) if incoming else s
         return pltpu.make_async_remote_copy(
-            src_ref=w_hbm.at[r],
-            dst_ref=wbuf.at[r, block],
-            send_sem=wsend_sem.at[o],
-            recv_sem=wrecv_sem.at[o],
+            src_ref=w_hbm.at[r, :, cols],
+            dst_ref=wbuf.at[r, block, :, cols],
+            send_sem=wsend_sem.at[o, q],
+            recv_sem=wrecv_sem.at[o, q],
             device_id={"seq": to},
             device_id_type=MESH,
         )
 
-    for o in range(1, n_seq):
-        w_copy(o, False).start()
+    for q in range(wparts):
+        for o in range(1, n_seq):
+            w_copy(o, q, False).start()
+
+    at_low = c == 0
+    far = jnp.where(c < n_chan // 2, n_chan - 1, 0)
+    far_o = lax.rem(s + n_seq - far, n_seq)
+    inner = jnp.where(at_low, c + 1, c - 1)
+    outer = jnp.where(c == 1, c - 1, c + 1)
+
+    def f_copy(q):
+        cols = pl.ds(q * wpiece, wpiece)
+        return pltpu.make_async_remote_copy(
+            src_ref=wbuf.at[r, far, :, cols],
+            dst_ref=pbuf.at[r, :, cols],
+            send_sem=fsend_sem.at[q],
+            recv_sem=frecv_sem.at[q],
+            device_id={"chan": inner},
+            device_id_type=MESH,
+        )
+
+    def y_copy(p, q, incoming):
+        which = lax.rem(r + n_rep - p, n_rep) if incoming else r
+        place = pbuf.at[which, :, pl.ds(q * wpiece, wpiece)]
+        return pltpu.make_async_remote_copy(
+            src_ref=place,
+            dst_ref=place,
+            send_sem=ysend_sem.at[p, q],
+            recv_sem=yrecv_sem.at[p, q],
+            device_id={"rep": lax.rem(r + p, n_rep)},
+            device_id_type=MESH,
+        )
+
+    def p_copy(k):
+        span = pl.ds(k * group, group)
+        return pltpu.make_async_remote_copy(
+            src_ref=psend.at[span],
+            dst_ref=precv.at[span],
+            send_sem=psend_sem.at[k],
+            recv_sem=precv_sem.at[k],
+            device_id={"chan": outer},
+            device_id_type=MESH,
+        )
 
     def x_copy(o, p, incoming):
         block = lax.rem(s + n_seq - o, n_seq)
@@ -158,6 +204,11 @@
 
         lax.fori_loop(0, depth // piece, one, 0)
 
+    own_tok.wait()
+    for copy in own_w:
+        copy.wait()
+
+    reach = n_chan - 2 if proxied else n_chan - 1
     for d in range(1, n_chan - 1):
         for k in order:
             for way in range(2):
@@ -167,17 +218,31 @@
                 def _():
                     tok_copy(block, k, way, False).wait_recv()
 
-                    @pl.when(can_send(way))
+                    if d < reach:
+                        @pl.when(can_send(way))
+                        def _():
+                            tok_copy(block, k, way, False).start()
+
+        if d == 1 and proxied:
+            @pl.when(at_end)
+            def _():
+                for q in range(wparts):
+                    @pl.when(s != far)
                     def _():
-                        tok_copy(block, k, way, False).start()
+                        w_copy(far_o, q, True).wait_recv()
+
+                    f_copy(q).start()
 
     for o in range(1, n_seq):
-        w_copy(o, True).wait_recv()
+        for q in range(wparts):
+            if proxied:
+                @pl.when(jnp.logical_not(at_end & (far_o == o)))
+                def _():
+                    w_copy(o, q, True).wait_recv()
+            else:
+                w_copy(o, q, True).wait_recv()
         for p in range(1, n_rep):
             x_copy(o, p, False).start()
-    own_tok.wait()
-    for copy in own_w:
-        copy.wait()
 
     def early(h):
         def one(block, carry):
@@ -191,7 +256,38 @@
 
         lax.fori_loop(0, n_chan, one, 0)
 
+    def partial(h):
+        def one(i, carry):
+            cols = pl.ds(pl.multiple_of(i * piece, piece), piece)
+            outs = pl.ds(pl.multiple_of(h * half, 128), half)
+            pacc[:, outs] += lax.dot_general(
+                tokbuf[far, :, cols],
+                pbuf[h, :, cols],
+                (((1,), (1,)), ((), ())),
+                preferred_element_type=F32,
+            )
+            return carry
+
+        lax.fori_loop(0, depth // piece, one, 0)
+
     early(r)
+    if proxied:
+        @pl.when(jnp.logical_not(at_end))
+        def _():
+            pacc[...] = jnp.zeros_like(pacc)
+            for q in range(wparts):
+                f_copy(q).wait_recv()
+                for p in range(1, n_rep):
+                    y_copy(p, q, False).start()
+            partial(r)
+            for p in range(1, n_rep):
+                for q in range(wparts):
+                    y_copy(p, q, True).wait_recv()
+                partial(lax.rem(r + n_rep - p, n_rep))
+            for k in order:
+                span = pl.ds(k * group, group)
+                psend[span, :] = pacc[span, :].astype(BF16)
+                p_copy(k).start()
     for p in range(1, n_rep):
         for o in range(1, n_seq):
             x_copy(o, p, True).wait_recv()
@@ -212,10 +308,9 @@
         feats = []
         for g in range(3):
             window = qbuf[pl.ds(base + 8, STEP + 8), g * ch : (g + 1) * ch]
-            feat = taps_ref[g : g + 1] * window[8:]
+            feat = taps_ref[0, g : g + 1] * window[8:]
             for j in range(1, 3):
-                row = j * 3 + g
-                feat = feat + taps_ref[row : row + 1] * window[8 - j : 8 - j + STEP]
+                feat = feat + taps_ref[j, g : g + 1] * window[8 - j : 8 - j + STEP]
             feats.append(feat)
         z = (feats[1] * feats[2]).astype(BF16).astype(F32)
         query[pl.ds(base, STEP), :] = feats[0]
@@ -231,7 +326,12 @@
     per = group // STEP
     for k in order:
         span = pl.ds(k * group, group)
-        if n_chan > 1:
+        if proxied:
+            @pl.when(at_end)
+            def _():
+                p_copy(k).wait_recv()
+                acc[span, :] += precv[span, :].astype(F32)
+        elif n_chan > 1:
             for way in range(2):
                 block, there = source(way, n_chan - 1)
 
@@ -368,17 +468,33 @@
             @pl.when(there & can_send(way))
             def _():
                 for k in range(parts):
-                    tok_copy(block, k, way, d == 0).wait_send()
+                    if d < reach:
+                        tok_copy(block, k, way, d == 0).wait_send()
                     g_copy(block, k, way).wait_send()
 
     for o in range(1, n_seq):
-        w_copy(o, False).wait_send()
+        for q in range(wparts):
+            w_copy(o, q, False).wait_send()
         for p in range(1, n_rep):
             x_copy(o, p, False).wait_send()
 
         @pl.when(s + o < n_seq)
         def _():
             s_copy(o).wait_send()
+
+    if proxied:
+        @pl.when(at_end)
+        def _():
+            for q in range(wparts):
+                f_copy(q).wait_send()
+
+        @pl.when(jnp.logical_not(at_end))
+        def _():
+            for q in range(wparts):
+                for p in range(1, n_rep):
+                    y_copy(p, q, False).wait_send()
+            for k in range(parts):
+                p_copy(k).wait_send()
 
     @pl.when(s < n_seq - 1)
     def _():
@@ -395,7 +511,6 @@
     parts = 4
     half = branches * ch // n_rep
     w = w_in.transpose(1, 0, 2).reshape(n_rep, half, wdepth)
-    taps = short_taps.reshape(short_taps.shape[0] * branches, ch)
     dims = (n_seq, n_chan, n_rep, parts, piece, rows, ch)
     vmem = pl.BlockSpec(memory_space=pltpu.VMEM)
     hbm = pl.BlockSpec(memory_space=pl.ANY)
@@ -423,13 +538,23 @@
             pltpu.VMEM((STEP, STEP, ch), F32),
             pltpu.VMEM((n_chan, rows, ch), BF16),
             pltpu.VMEM((rows, width), F32),
+            pltpu.VMEM((n_rep, half, wdepth), BF16),
+            pltpu.VMEM((rows, branches * ch), F32),
+            pltpu.VMEM((rows, branches * ch), BF16),
+            pltpu.VMEM((rows, branches * ch), BF16),
             dma((2 + n_rep,)),
             dma((2, n_chan, parts)),
             dma((n_chan, parts)),
-            dma((n_seq,)),
-            dma((n_seq,)),
+            dma((n_seq, 4)),
+            dma((n_seq, 4)),
             dma((n_seq, n_rep)),
             dma((n_seq, n_rep)),
+            dma((4,)),
+            dma((4,)),
+            dma((n_rep, 4)),
+            dma((n_rep, 4)),
+            dma((parts,)),
+            dma((parts,)),
             dma(()),
             dma(()),
             dma((n_seq,)),
@@ -445,7 +570,7 @@
             bytes_accessed=2 * (rows * depth + branches * ch * wdepth + n_chan * ch * width),
             transcendentals=0,
         ),
-    )(tokens, w, taps, decay, residue, skip.reshape(1, ch), w_out.reshape(n_chan, ch, width))
+    )(tokens, w, short_taps, decay, residue, skip.reshape(1, ch), w_out.reshape(n_chan, ch, width))
 
 
 def solution(mesh):

time: 133 us -> 123 us (0.925)
  Pallas kernels: 128 us -> 120 us
    pallas_call x1, Pallas kernels: 128 us -> 120 us  [on_device(): pl.pallas_call(functools.partial(kernel, dims), out_shape=jax.ShapeDtypeS...]
where the time goes in v2:
time: 123 us; the launch traced here: 122 us
  Pallas kernels  120 us (98%)
  local copies, waits for them, and re-layouts  2.73 us (2%)
    pallas_call x1, Pallas kernels, on_device(): pl.pallas_call(functools.partial(kernel, dims), out_shape=jax.ShapeDtypeS...  120 us
    unnamed x1, local copies, waits for them, and re-layouts  2.73 us

profile of v2, /device:TPU:4, one launch (start us, length us, event | category | flops | bytes accessed | tf_op | source)
XLA Modules:
  0.0 122.3 jit_solution(5885428881365669965)
XLA Ops:
  0.0 119.6 %shard_map.73 = bf16[384,2048]{1,0:T(8,128)(2,1)} custom-call(bf16[384,2048]{1,0:T(8,128)(2,1)} %tok_hbm.1, bf16[2,384,2048]{2,1,0:T(8,128)(2,1)} %bitcast.6, f32[3,3,256]{2,1,0:T(4,128)} %taps_ref.1, f32[16,256]{1,0:T(8,128)} %decay_ref.1, f32[16,256]{1,0:T(8,128)} %residue_ref.1, f32[1,256]{1,0:T(1,128)} %bitcast.7, bf16[4,256,2048]{2,1,0:T(8,128)(2,1)} %bitcast.5), custom_call_target="tpu_custom_call" | custom-call | flops 6442450944 | bytes 8912896 | tf_op jit(solution)/shard_map/pallas_call | solution.py:518
  119.6 2.7 %copy.9 = bf16[384,2048]{1,0:T(8,128)(2,1)} copy(bf16[384,2048]{1,0:T(8,128)(2,1)} %shard_map.73) | data formatting | bytes 3145728

commit v3 on v2

--- a/solution.py
+++ b/solution.py
@@ -102,10 +102,27 @@
             def _():
                 tok_copy(c, k, way, True).start()
 
+    def partner(o):
+        if proxied:
+            flips = (s + 1 - 2 * lax.rem(s, 2), s + 2 - 4 * (s // 2), 3 - s)
+            return flips[abs(o) - 1]
+        return lax.rem(s + n_seq + o, n_seq)
+
+    def relay(q):
+        place = wbuf.at[r, partner(1 + q % 2), :, pl.ds(q * wpiece, wpiece)]
+        return pltpu.make_async_remote_copy(
+            src_ref=place,
+            dst_ref=place,
+            send_sem=wsend_sem.at[3, q],
+            recv_sem=wrecv_sem.at[3, q],
+            device_id={"seq": partner(2 - q % 2)},
+            device_id_type=MESH,
+        )
+
     def w_copy(o, q, incoming):
         cols = pl.ds(q * wpiece, wpiece)
-        to = lax.rem(s + o, n_seq)
-        block = lax.rem(s + n_seq - o, n_seq) if incoming else s
+        to = partner(o)
+        block = partner(-o) if incoming else s
         return pltpu.make_async_remote_copy(
             src_ref=w_hbm.at[r, :, cols],
             dst_ref=wbuf.at[r, block, :, cols],
@@ -116,12 +133,12 @@
         )
 
     for q in range(wparts):
-        for o in range(1, n_seq):
+        for o in range(1, 3 if proxied else n_seq):
             w_copy(o, q, False).start()
 
     at_low = c == 0
     far = jnp.where(c < n_chan // 2, n_chan - 1, 0)
-    far_o = lax.rem(s + n_seq - far, n_seq)
+    late = at_end & (s + far == 3)
     inner = jnp.where(at_low, c + 1, c - 1)
     outer = jnp.where(c == 1, c - 1, c + 1)
 
@@ -160,7 +177,7 @@
         )
 
     def x_copy(o, p, incoming):
-        block = lax.rem(s + n_seq - o, n_seq)
+        block = partner(-o)
         which = lax.rem(r + n_rep - p, n_rep) if incoming else r
         place = wbuf.at[which, block]
         return pltpu.make_async_remote_copy(
@@ -223,22 +240,30 @@
                         def _():
                             tok_copy(block, k, way, False).start()
 
+            if d == 1 and proxied:
+                q = order.index(k)
+                w_copy(1, q, True).wait_recv()
+                w_copy(2, q, True).wait_recv()
+                relay(q).start()
+
+                @pl.when(at_end & jnp.logical_not(late))
+                def _():
+                    f_copy(q).start()
+
         if d == 1 and proxied:
-            @pl.when(at_end)
+            @pl.when(late)
             def _():
                 for q in range(wparts):
-                    @pl.when(s != far)
-                    def _():
-                        w_copy(far_o, q, True).wait_recv()
-
+                    w_copy(3, q, True).wait_recv()
                     f_copy(q).start()
 
     for o in range(1, n_seq):
         for q in range(wparts):
             if proxied:
-                @pl.when(jnp.logical_not(at_end & (far_o == o)))
-                def _():
-                    w_copy(o, q, True).wait_recv()
+                if o == 3:
+                    @pl.when(jnp.logical_not(late))
+                    def _():
+                        w_copy(o, q, True).wait_recv()
             else:
                 w_copy(o, q, True).wait_recv()
         for p in range(1, n_rep):
@@ -474,7 +499,7 @@
 
     for o in range(1, n_seq):
         for q in range(wparts):
-            w_copy(o, q, False).wait_send()
+            (relay(q) if proxied and o == 3 else w_copy(o, q, False)).wait_send()
         for p in range(1, n_rep):
             x_copy(o, p, False).wait_send()
 

time: 123 us -> 123 us (level)
  no operation moved by 1% of the time
where the time goes in v3:
time: 123 us
  Pallas kernels  120 us (98%)
  local copies, waits for them, and re-layouts  2.73 us (2%)
    pallas_call x1, Pallas kernels, on_device(): pl.pallas_call(functools.partial(kernel, dims), out_shape=jax.ShapeDtypeS...  120 us
    unnamed x1, local copies, waits for them, and re-layouts  2.73 us

profile of v3, /device:TPU:4, one launch (start us, length us, event | category | flops | bytes accessed | tf_op | source)
XLA Modules:
  0.0 122.6 jit_solution(15786062190146545779)
XLA Ops:
  0.0 119.9 %shard_map.73 = bf16[384,2048]{1,0:T(8,128)(2,1)} custom-call(bf16[384,2048]{1,0:T(8,128)(2,1)} %tok_hbm.1, bf16[2,384,2048]{2,1,0:T(8,128)(2,1)} %bitcast.6, f32[3,3,256]{2,1,0:T(4,128)} %taps_ref.1, f32[16,256]{1,0:T(8,128)} %decay_ref.1, f32[16,256]{1,0:T(8,128)} %residue_ref.1, f32[1,256]{1,0:T(1,128)} %bitcast.7, bf16[4,256,2048]{2,1,0:T(8,128)(2,1)} %bitcast.5), custom_call_target="tpu_custom_call" | custom-call | flops 6442450944 | bytes 8912896 | tf_op jit(solution)/shard_map/pallas_call | solution.py:543
  119.9 2.7 %copy.9 = bf16[384,2048]{1,0:T(8,128)(2,1)} copy(bf16[384,2048]{1,0:T(8,128)(2,1)} %shard_map.73) | data formatting | bytes 3145728

commit v4 on v3

--- a/solution.py
+++ b/solution.py
@@ -295,7 +295,6 @@
 
         lax.fori_loop(0, depth // piece, one, 0)
 
-    early(r)
     if proxied:
         @pl.when(jnp.logical_not(at_end))
         def _():
@@ -313,6 +312,8 @@
                 span = pl.ds(k * group, group)
                 psend[span, :] = pacc[span, :].astype(BF16)
                 p_copy(k).start()
+
+    early(r)
     for p in range(1, n_rep):
         for o in range(1, n_seq):
             x_copy(o, p, True).wait_recv()

time: 123 us -> 125 us (1.016)
  Pallas kernels: 120 us -> 122 us
    pallas_call x1, Pallas kernels: 120 us -> 122 us  [on_device(): pl.pallas_call(functools.partial(kernel, dims), out_shape=jax.ShapeDtypeS...]
where the time goes in v4:
time: 125 us
  Pallas kernels  122 us (98%)
  local copies, waits for them, and re-layouts  2.73 us (2%)
    pallas_call x1, Pallas kernels, on_device(): pl.pallas_call(functools.partial(kernel, dims), out_shape=jax.ShapeDtypeS...  122 us
    unnamed x1, local copies, waits for them, and re-layouts  2.73 us

profile of v4, /device:TPU:4, one launch (start us, length us, event | category | flops | bytes accessed | tf_op | source)
XLA Modules:
  0.0 125.2 jit_solution(10110710569859053295)
XLA Ops:
  0.0 122.5 %shard_map.73 = bf16[384,2048]{1,0:T(8,128)(2,1)} custom-call(bf16[384,2048]{1,0:T(8,128)(2,1)} %tok_hbm.1, bf16[2,384,2048]{2,1,0:T(8,128)(2,1)} %bitcast.6, f32[3,3,256]{2,1,0:T(4,128)} %taps_ref.1, f32[16,256]{1,0:T(8,128)} %decay_ref.1, f32[16,256]{1,0:T(8,128)} %residue_ref.1, f32[1,256]{1,0:T(1,128)} %bitcast.7, bf16[4,256,2048]{2,1,0:T(8,128)(2,1)} %bitcast.5), custom_call_target="tpu_custom_call" | custom-call | flops 6442450944 | bytes 8912896 | tf_op jit(solution)/shard_map/pallas_call | solution.py:544
  122.5 2.7 %copy.9 = bf16[384,2048]{1,0:T(8,128)(2,1)} copy(bf16[384,2048]{1,0:T(8,128)(2,1)} %shard_map.73) | data formatting | bytes 3145728
